TPU v7x, 32 devices: a whole 2x2x4 slice. The times are simulated.
32 devices in a mesh: pipe: 4 (over x, core), dp: 2 (over y), vocab: 4 (over z).
Axes of the slice: x: 2, y: 2, z: 4, core: 2. Of those that a mesh axis runs over, the one named last changes fastest.
Arguments:
- hidden: bfloat16 [512, 4608], P(('pipe', 'dp', 'vocab')), may hold values from -6 to 6
- targets: int32 [512], P(('pipe', 'dp', 'vocab')), may hold values from 0 to 12287, as said below
- input_ids: int32 [512], P(('pipe', 'dp', 'vocab')), may hold values from 0 to 12287, as said below
- input_grads: bfloat16 [512, 4608], P(('pipe', 'dp', 'vocab')), may hold values from -0.3125 to 0.3125
- table: bfloat16 [12288, 4608], P(('pipe', 'vocab'), 'dp'), may hold values from -0.75 to 0.75
- keep: int32 [12288], P(('pipe', 'vocab')), may hold values from 0 to 1
- first_moment: bfloat16 [12288, 4608], P(('pipe', 'vocab'), 'dp'), may hold values from -0.015625 to 0.015625
- second_moment: bfloat16 [12288, 4608], P(('pipe', 'vocab'), 'dp'), may hold values from 9.983778e-07 to 9.953976e-06
Outputs:
- new_table: bfloat16 [12288, 4608], P(('pipe', 'vocab'), 'dp')
- new_first: bfloat16 [12288, 4608], P(('pipe', 'vocab'), 'dp')
- new_second: bfloat16 [12288, 4608], P(('pipe', 'vocab'), 'dp')
- loss: float32 [], replicated
Inputs may be any that keep to these rules, and one draw needn't show every extreme that they name: `targets`: names only rows with keep = 1. `input_ids`: names only rows with keep = 1.
All inputs are finite; a program needn't handle non-finite values.
Results may differ from a plain program's by a relative error of at most 0.0036.
Values may be sent and summed in bfloat16 or wider, within the bound.
A program may use at most 192 MiB of HBM per device.

v0:
```python
import math
import jax
import jax.numpy as jnp
from jax import lax
from jax.sharding import PartitionSpec as P

SOFTCAP = 30.0
LEARN = 0.01
EPSILON = 1e-08


def contract_last(left, right):
    return lax.dot_general(
        left, right, (((1,), (1,)), ((), ())), preferred_element_type=jnp.float32
    )


def contract_first(left, right):
    return lax.dot_general(
        left, right, (((0,), (0,)), ((), ())), preferred_element_type=jnp.float32
    )


def body(hidden, targets, input_ids, input_grads, table, keep, first_moment, second_moment):
    rows_here = table.shape[0]
    row_start = lax.axis_index(("pipe", "vocab")) * rows_here
    keepf = keep.astype(jnp.float32)
    scale = math.sqrt(hidden.shape[1])
    groups_dp = lax.axis_size("dp")
    row_iota = jnp.arange(rows_here, dtype=jnp.int32)
    both = jnp.stack([targets, input_ids])
    packed = lax.all_to_all(
        jnp.stack([hidden, input_grads]), "dp", split_axis=2, concat_axis=1, tiled=True
    )
    ids_all = lax.all_gather(both, ("pipe", "vocab", "dp"), axis=1, tiled=True)
    tokens_all = lax.all_gather(packed[0], ("pipe", "vocab"), axis=0, tiled=True)
    grads_all = lax.all_gather(packed[1], ("pipe", "vocab"), axis=0, tiled=True)
    tokens = tokens_all.shape[0]
    share = tokens // groups_dp
    start = lax.axis_index("dp") * share
    goals = lax.dynamic_slice(ids_all[0], (start,), (share,))
    raw = lax.psum_scatter(contract_last(tokens_all, table), "dp", scatter_dimension=0, tiled=True)
    capped = SOFTCAP * jnp.tanh(raw / SOFTCAP)
    onehot = ((goals - row_start)[:, None] == row_iota[None, :]).astype(jnp.float32)
    weights = jnp.exp(capped) * keepf[None, :]
    local = jnp.stack([jnp.sum(weights, axis=1), jnp.sum(capped * onehot, axis=1)])
    placed = lax.dynamic_update_slice(jnp.zeros((2, tokens), jnp.float32), local, (0, start))
    sums = lax.psum(placed, ("pipe", "dp", "vocab"))
    token_loss = jnp.sum(jnp.log(sums[0]) - sums[1])
    total = lax.dynamic_slice(sums[0], (start,), (share,))
    slope = 1.0 - (capped / SOFTCAP) ** 2
    dlogits = ((weights / total[:, None] - onehot) * slope).astype(jnp.bfloat16)
    dlogits = lax.all_gather(dlogits, "dp", axis=0, tiled=True)
    selector = ((ids_all[1] - row_start)[None, :] == row_iota[:, None]).astype(jnp.bfloat16)
    finished = contract_first(dlogits, tokens_all) + scale * jnp.dot(
        selector, grads_all, preferred_element_type=jnp.float32
    )
    kept = keep[:, None] > 0
    first_new = (0.9 * first_moment.astype(jnp.float32) + 0.1 * finished).astype(jnp.bfloat16)
    second_new = (0.95 * second_moment.astype(jnp.float32) + 0.05 * finished * finished).astype(
        jnp.bfloat16
    )
    corr_one = 1.0 - 0.9**10
    corr_two = 1.0 - 0.95**10
    update = (
        first_new.astype(jnp.float32)
        / corr_one
        / (jnp.sqrt(second_new.astype(jnp.float32) / corr_two) + EPSILON)
    )
    table_new = (table.astype(jnp.float32) - LEARN * update).astype(jnp.bfloat16)
    new_table = jnp.where(kept, table_new, table)
    new_first = jnp.where(kept, first_new, first_moment)
    new_second = jnp.where(kept, second_new, second_moment)
    return (new_table, new_first, new_second, token_loss)


def solution(mesh):
    placed = (
        P(("pipe", "dp", "vocab"), None),
        P(("pipe", "dp", "vocab")),
        P(("pipe", "dp", "vocab")),
        P(("pipe", "dp", "vocab"), None),
        P(("pipe", "vocab"), "dp"),
        P(("pipe", "vocab")),
        P(("pipe", "vocab"), "dp"),
        P(("pipe", "vocab"), "dp"),
    )
    return jax.shard_map(
        body,
        mesh=mesh,
        in_specs=placed,
        out_specs=(
            P(("pipe", "vocab"), "dp"),
            P(("pipe", "vocab"), "dp"),
            P(("pipe", "vocab"), "dp"),
            P(),
        ),
        check_vma=False,
    )
```

profile of v0, /device:TPU:10, one launch (start us, length us, event | category | flops | bytes accessed | tf_op | source)
XLA Modules:
  0.0 227.2 jit_solution(489731304706484116)
XLA Ops:
  7.2 0.0 all-gather.4.cloned.1.call-start
  7.2 1.0 pad_maximum_fusion
  8.2 3.0 %copy.27 = bf16[2,16,4608]{1,0,2:T(2,128)(2,1)S(1)} copy(bf16[2,16,4608]{2,1,0:T(8,128)(2,1)S(1)} %pad_maximum_fusion) | data formatting | bytes 589824 | tf_op jit(solution)/shard_map/stack | solution.py:33
  11.2 2.5 %reshape.30 = bf16[2,2,36864]{2,1,0:T(2,128)(2,1)S(1)} reshape(bf16[4608,2,16]{2,1,0:T(2,128)(2,1)S(1)} %bitcast.27) | data formatting | bytes 589824
  13.7 8.2 %all_to_all.15 = bf16[2,2,36864]{2,1,0:T(2,128)(2,1)S(1)} all-to-all(bf16[2,2,36864]{2,1,0:T(2,128)(2,1)S(1)} %reshape.30), channel_id=1, replica_groups=mesh['pipe'=4,'dp'=2,'vocab'=4] {'dp'}, dimensions={0} | all-to-all | bytes 589824 | tf_op jit(solution)/shard_map/all_to_all | solution.py:32
  21.9 1.6 reshape.31
  23.5 1.6 copy.32
  25.1 0.2 fusion.6
  25.3 0.7 copy.29
  26.0 0.0 all-gather.4.cloned.1.call-update
  26.0 0.0 copy-start.1
  26.0 0.0 copy-start.2
  26.0 0.0 copy-start.3
  26.1 0.0 reduce-scatter.2.cloned.1.call-start
  26.1 41.0 %all-gather.4.cloned.1.call-done = bf16[512,2304]{1,0:T(8,128)(2,1)} async-done(((bf16[32,2304]{1,0:T(8,128)(2,1)}), bf16[512,2304]{1,0:T(8,128)(2,1)}) %all-gather.4.cloned.1.call-update) | async-done | bytes 2359312 | tf_op jit(solution)/shard_map/all_gather | solution.py:36
  67.2 5.9 %fusion.7 = f32[512,768]{1,0:T(8,128)} fusion(bf16[512,2304]{1,0:T(8,128)(2,1)} %all-gather.4.cloned.1.call-done, bf16[768,2304]{1,0:T(8,128)(2,1)} %param.12), kind=kOutput, calls=%fused_computation.27 | convolution fusion | flops 1811939328 | bytes 7471104 | tf_op jit(solution)/shard_map/dot_general | solution.py:13
  73.0 0.0 copy-start
  73.0 0.0 reduce-scatter.2.cloned.1.call-update
  73.1 0.0 all-gather.6.cloned.1.call-start
  73.1 0.7 copy.31
  73.8 0.0 all-gather.6.cloned.1.call-update
  73.8 0.0 copy-done.1
  73.8 0.0 copy-done.2
  73.9 0.0 copy-done.3
  73.9 65.0 %all-gather = s32[32,16,2]{1,2,0:T(2,128)S(1)} all-gather(s32[1,16,2]{1,2,0:T(2,128)S(1)} %add_bitcast_fusion), channel_id=1, replica_groups=mesh['pipe'=4,'dp'=2,'vocab'=4] {'pipe','vocab','dp'}, dimensions={0}, use_global_device_ids=true | all-gather | bytes 4224 | tf_op jit(solution)/shard_map/all_gather | solution.py:35
  138.8 0.1 reshape.29
  139.0 0.0 reduce-scatter.2.cloned.1.call-done
  139.0 1.6 fusion.4
  140.7 42.0 %psum.7 = f32[2,512]{1,0:T(2,128)S(1)} all-reduce(f32[2,512]{1,0:T(2,128)S(1)} %maximum_dynamic-update-slice_fusion), channel_id=1, replica_groups=mesh['pipe'=4,'dp'=2,'vocab'=4] {'pipe','dp','vocab'}, use_global_device_ids=true, to_apply=%region_3.0 | all-reduce | flops 1024 | bytes 8192 | tf_op jit(solution)/shard_map/psum | solution.py:48
  182.6 0.6 fusion.5
  183.2 1.5 multiply_convert_fusion
  184.8 10.6 %all_gather.14 = bf16[512,768]{1,0:T(8,128)(2,1)S(1)} all-gather(bf16[256,768]{1,0:T(8,128)(2,1)S(1)} %multiply_convert_fusion), channel_id=1, replica_groups=mesh['pipe'=4,'dp'=2,'vocab'=4] {'dp'}, dimensions={0}, use_global_device_ids=true | all-gather | bytes 1179648 | tf_op jit(solution)/shard_map/all_gather | solution.py:53
  195.4 0.0 copy-done
  195.4 5.0 %fusion.8 = f32[768,2304]{1,0:T(8,128)} fusion(bf16[512,768]{1,0:T(8,128)(2,1)S(1)} %all_gather.14, bf16[512,2304]{1,0:T(8,128)(2,1)S(1)} %copy-done), kind=kOutput, calls=%fused_computation.28 | convolution fusion | flops 1811939328 | bytes 10223616 | tf_op jit(solution)/shard_map/dot_general | solution.py:19
  200.4 0.0 all-gather.6.cloned.1.call-done
  200.4 20.3 %broadcast_select_fusion = (bf16[768,2304]{1,0:T(8,128)(2,1)}, bf16[768,2304]{1,0:T(8,128)(2,1)}, bf16[768,2304]{1,0:T(8,128)(2,1)}) fusion(bf16[768,2304]{1,0:T(8,128)(2,1)} %param.15, pred[768]{0:T(1024)(128)(4,1)S(1)} %broadcast_compare_fusion, bf16[768,2304]{1,0:T(8,128)(2,1)} %param.12, bf16[768,2304]{1,0:T(8,128)(2,1)} %param.14, ...), kind=kOutput, calls=%fused_computation.7 | convolution fusion | flops 1858338816 | bytes 30673664 | tf_op jit(solution)/shard_map/dot_general | solution.py:55
  (9 shorter events, 0.1 us)
Async XLA Ops:
  7.2 60.0 %all-gather.4.cloned.1.call-start = ((), (), s32[]{:S(2)}) async-start(), calls=%async_computation.2 | async-start | bytes 2506752 | tf_op jit(solution)/shard_map/all_gather | solution.py:36
  26.0 47.8 %copy-start.1 = (s32[768]{0:T(1024)S(1)}, s32[768]{0:T(1024)}, u32[]{:S(2)}) copy-start(s32[768]{0:T(1024)} %param.13) | copy-start | bytes 9220
  26.0 47.8 %copy-start.2 = (s32[16]{0:T(128)S(1)}, s32[16]{0:T(128)}, u32[]{:S(2)}) copy-start(s32[16]{0:T(128)} %param.10) | copy-start | bytes 196
  26.0 47.8 %copy-start.3 = (s32[16]{0:T(128)S(1)}, s32[16]{0:T(128)}, u32[]{:S(2)}) copy-start(s32[16]{0:T(128)} %param.9) | copy-start | bytes 196
  26.1 113.0 %reduce-scatter.2.cloned.1.call-start = ((), (), s32[]{:S(2)}) async-start(), calls=%async_computation.3 | async-start | bytes 2359296 | tf_op jit(solution)/shard_map/reduce_scatter | solution.py:42
  73.0 122.4 %copy-start = (bf16[512,2304]{1,0:T(8,128)(2,1)S(1)}, bf16[512,2304]{1,0:T(8,128)(2,1)}, u32[]{:S(2)}) copy-start(bf16[512,2304]{1,0:T(8,128)(2,1)} %all-gather.4.cloned.1.call-done) | copy-start | bytes 7077892
  73.1 127.3 %all-gather.6.cloned.1.call-start = ((), (), s32[]{:S(2)}) async-start(), calls=%async_computation.4 | async-start | bytes 2506752 | tf_op jit(solution)/shard_map/all_gather | solution.py:37
Sparse Core Ops, SparseCore 0:
  26.1 40.9 all-gather.3
  73.2 26.5 reduce-scatter.1
  102.9 40.8 all-gather.5
where the time goes:
time: 228 us; the launch traced here: 227 us
  blocking collectives  126 us (55%)
  waiting for transfers between devices  41.1 us (18%)
  matrix products  31.1 us (14%)
  between operations  13.9 us (6%)
  local copies, waits for them, and re-layouts  10.4 us (5%)
  other arithmetic  4.81 us (2%)
    all_gather x1, blocking collectives, body(): ids_all = lax.all_gather(both, ('pipe', 'vocab', 'dp'), axis=1, tiled=True)  65 us
    psum x1, blocking collectives, body(): sums = lax.psum(placed, ('pipe', 'dp', 'vocab'))  42 us
    all_gather x1, waiting for transfers between devices, body(): lax.all_gather(packed[0], ('pipe', 'vocab'), axis=0, tiled=True)  41 us
    dot_general x1, matrix products, body(): jnp.dot(selector, grads_all, preferred_element_type=jnp.float32)  20.3 us
    all_gather x1, blocking collectives, body(): dlogits = lax.all_gather(dlogits, 'dp', axis=0, tiled=True)  10.6 us
    all_to_all x1, blocking collectives, body(): lax.all_to_all(jnp.stack([hidden, input_grads]), 'dp', split_axis=2, conc...  8.17 us
    dot_general x1, matrix products, contract_last(): lax.dot_general(left, right, (((1,), (1,)), ((), ())), preferred_element_...  5.88 us
    dot_general x1, matrix products, contract_first(): lax.dot_general(left, right, (((0,), (0,)), ((), ())), preferred_element_...  4.95 us
  transfers between devices with their start and end apart: 3, of which 1 were waited for; matrix products, arithmetic and copies ran while one was open for 4% of the time, Pallas kernels for 0%

commit v1 on v0

--- a/solution.py
+++ b/solution.py
@@ -29,8 +29,14 @@
     groups_dp = lax.axis_size("dp")
     row_iota = jnp.arange(rows_here, dtype=jnp.int32)
     both = jnp.stack([targets, input_ids])
-    packed = lax.all_to_all(
-        jnp.stack([hidden, input_grads]), "dp", split_axis=2, concat_axis=1, tiled=True
+    packed = jnp.concatenate(
+        lax.all_to_all(
+            jnp.stack(jnp.split(jnp.stack([hidden, input_grads]), lax.axis_size("dp"), axis=2)),
+            "dp",
+            0,
+            0,
+        ),
+        axis=1,
     )
     ids_all = lax.all_gather(both, ("pipe", "vocab", "dp"), axis=1, tiled=True)
     tokens_all = lax.all_gather(packed[0], ("pipe", "vocab"), axis=0, tiled=True)

time: 228 us -> 219 us (0.961)
  local copies, waits for them, and re-layouts: 10.4 us -> 0.85 us
    unnamed x11 -> x9, local copies, waits for them, and re-layouts: 4.16 us -> 0.11 us
    another operation x1 -> x0, local copies, waits for them, and re-layouts: 3.01 us -> none  [body(): jnp.stack([hidden, input_grads])]
where the time goes in v1:
time: 219 us
  blocking collectives  126 us (58%)
  waiting for transfers between devices  41.8 us (19%)
  matrix products  31.3 us (14%)
  between operations  13.9 us (6%)
  other arithmetic  4.85 us (2%)
    all_gather x1, blocking collectives, body(): ids_all = lax.all_gather(both, ('pipe', 'vocab', 'dp'), axis=1, tiled=True)  65 us
    psum x1, blocking collectives, body(): sums = lax.psum(placed, ('pipe', 'dp', 'vocab'))  42 us
    all_gather x1, waiting for transfers between devices, body(): lax.all_gather(packed[0], ('pipe', 'vocab'), axis=0, tiled=True)  41 us
    dot_general x1, matrix products, body(): jnp.dot(selector, grads_all, preferred_element_type=jnp.float32)  20.3 us
    all_gather x1, blocking collectives, body(): dlogits = lax.all_gather(dlogits, 'dp', axis=0, tiled=True)  10.6 us
    all_to_all x1, blocking collectives, body(): lax.all_to_all(jnp.stack(jnp.split(jnp.stack([hidden, input_grads]), lax....  8.17 us
    dot_general x1, matrix products, contract_last(): lax.dot_general(left, right, (((1,), (1,)), ((), ())), preferred_element_...  6.03 us
    dot_general x1, matrix products, contract_first(): lax.dot_general(left, right, (((0,), (0,)), ((), ())), preferred_element_...  4.95 us
  transfers between devices with their start and end apart: 3, of which 1 were waited for; matrix products, arithmetic and copies ran while one was open for 4% of the time, Pallas kernels for 0%

profile of v1, /device:TPU:10, one launch (start us, length us, event | category | flops | bytes accessed | tf_op | source)
XLA Modules:
  0.0 218.5 jit_solution(3205965546625914724)
XLA Ops:
  7.2 0.0 all-gather.4.cloned.1.call-start
  7.2 1.0 fusion.6
  8.3 8.2 %all_to_all.5 = bf16[2,2,16,2304]{3,2,1,0:T(8,128)(2,1)S(1)} all-to-all(bf16[2,2,16,2304]{3,2,1,0:T(8,128)(2,1)S(1)} %pad_maximum_fusion), channel_id=1, replica_groups=mesh['pipe'=4,'dp'=2,'vocab'=4] {'dp'}, dimensions={0} | all-to-all | bytes 589824 | tf_op jit(solution)/shard_map/all_to_all | solution.py:33
  16.4 0.7 fusion.9
  17.2 0.0 all-gather.4.cloned.1.call-update
  17.2 0.0 copy-start.1
  17.2 0.0 copy-start.2
  17.2 0.0 copy-start.3
  17.2 0.0 reduce-scatter.2.cloned.1.call-start
  17.3 41.0 %all-gather.4.cloned.1.call-done = bf16[512,2304]{1,0:T(8,128)(2,1)} async-done(((bf16[32,2304]{1,0:T(8,128)(2,1)}), bf16[512,2304]{1,0:T(8,128)(2,1)}) %all-gather.4.cloned.1.call-update) | async-done | bytes 2359312 | tf_op jit(solution)/shard_map/all_gather | solution.py:42
  58.3 0.0 copy-start
  58.3 6.0 %fusion.10 = f32[512,768]{1,0:T(8,128)} fusion(bf16[512,2304]{1,0:T(8,128)(2,1)} %all-gather.4.cloned.1.call-done, bf16[768,2304]{1,0:T(8,128)(2,1)} %param.12), kind=kOutput, calls=%fused_computation.33 | convolution fusion | flops 1811939328 | bytes 7471104 | tf_op jit(solution)/shard_map/dot_general | solution.py:13
  64.4 0.0 reduce-scatter.2.cloned.1.call-update
  64.4 0.0 all-gather.6.cloned.1.call-start
  64.4 0.7 all-gather.6.cloned.1.call-update
  65.1 0.0 copy-done.1
  65.1 0.0 copy-done.2
  65.2 0.0 copy-done.3
  65.2 65.0 %all-gather = s32[32,16,2]{1,2,0:T(2,128)S(1)} all-gather(s32[1,16,2]{1,2,0:T(2,128)S(1)} %add_bitcast_fusion), channel_id=1, replica_groups=mesh['pipe'=4,'dp'=2,'vocab'=4] {'pipe','vocab','dp'}, dimensions={0}, use_global_device_ids=true | all-gather | bytes 4224 | tf_op jit(solution)/shard_map/all_gather | solution.py:41
  130.1 0.1 reshape.34
  130.3 0.0 reduce-scatter.2.cloned.1.call-done
  130.3 1.6 fusion.4
  132.0 42.0 %psum.7 = f32[2,512]{1,0:T(2,128)S(1)} all-reduce(f32[2,512]{1,0:T(2,128)S(1)} %maximum_dynamic-update-slice_fusion), channel_id=1, replica_groups=mesh['pipe'=4,'dp'=2,'vocab'=4] {'pipe','dp','vocab'}, use_global_device_ids=true, to_apply=%region_3.0 | all-reduce | flops 1024 | bytes 8192 | tf_op jit(solution)/shard_map/psum | solution.py:54
  173.9 0.6 fusion.8
  174.5 1.5 multiply_convert_fusion
  176.1 10.6 %all_gather.14 = bf16[512,768]{1,0:T(8,128)(2,1)S(1)} all-gather(bf16[256,768]{1,0:T(8,128)(2,1)S(1)} %multiply_convert_fusion), channel_id=1, replica_groups=mesh['pipe'=4,'dp'=2,'vocab'=4] {'dp'}, dimensions={0}, use_global_device_ids=true | all-gather | bytes 1179648 | tf_op jit(solution)/shard_map/all_gather | solution.py:59
  186.7 0.0 copy-done
  186.7 4.9 %fusion.11 = f32[768,2304]{1,0:T(8,128)} fusion(bf16[512,768]{1,0:T(8,128)(2,1)S(1)} %all_gather.14, bf16[512,2304]{1,0:T(8,128)(2,1)S(1)} %copy-done), kind=kOutput, calls=%fused_computation.34 | convolution fusion | flops 1811939328 | bytes 10223616 | tf_op jit(solution)/shard_map/dot_general | solution.py:19
  191.7 0.0 all-gather.6.cloned.1.call-done
  191.7 20.3 %broadcast_select_fusion = (bf16[768,2304]{1,0:T(8,128)(2,1)}, bf16[768,2304]{1,0:T(8,128)(2,1)}, bf16[768,2304]{1,0:T(8,128)(2,1)}) fusion(bf16[768,2304]{1,0:T(8,128)(2,1)} %param.15, pred[768]{0:T(1024)(128)(4,1)S(1)} %broadcast_compare_fusion, bf16[768,2304]{1,0:T(8,128)(2,1)} %param.12, bf16[768,2304]{1,0:T(8,128)(2,1)} %param.14, ...), kind=kOutput, calls=%fused_computation.7 | convolution fusion | flops 1858338816 | bytes 30673664 | tf_op jit(solution)/shard_map/dot_general | solution.py:61
  (10 shorter events, 0.1 us)
Async XLA Ops:
  7.2 51.2 %all-gather.4.cloned.1.call-start = ((), (), s32[]{:S(2)}) async-start(), calls=%async_computation.2 | async-start | bytes 2506752 | tf_op jit(solution)/shard_map/all_gather | solution.py:42
  17.2 47.9 %copy-start.1 = (s32[768]{0:T(1024)S(1)}, s32[768]{0:T(1024)}, u32[]{:S(2)}) copy-start(s32[768]{0:T(1024)} %param.13) | copy-start | bytes 9220
  17.2 47.9 %copy-start.2 = (s32[16]{0:T(128)S(1)}, s32[16]{0:T(128)}, u32[]{:S(2)}) copy-start(s32[16]{0:T(128)} %param.10) | copy-start | bytes 196
  17.2 47.9 %copy-start.3 = (s32[16]{0:T(128)S(1)}, s32[16]{0:T(128)}, u32[]{:S(2)}) copy-start(s32[16]{0:T(128)} %param.9) | copy-start | bytes 196
  17.2 113.1 %reduce-scatter.2.cloned.1.call-start = ((), (), s32[]{:S(2)}) async-start(), calls=%async_computation.3 | async-start | bytes 2359296 | tf_op jit(solution)/shard_map/reduce_scatter | solution.py:48
  58.3 128.4 %copy-start = (bf16[512,2304]{1,0:T(8,128)(2,1)S(1)}, bf16[512,2304]{1,0:T(8,128)(2,1)}, u32[]{:S(2)}) copy-start(bf16[512,2304]{1,0:T(8,128)(2,1)} %all-gather.4.cloned.1.call-done) | copy-start | bytes 7077892
  64.4 127.3 %all-gather.6.cloned.1.call-start = ((), (), s32[]{:S(2)}) async-start(), calls=%async_computation.4 | async-start | bytes 2506752 | tf_op jit(solution)/shard_map/all_gather | solution.py:43
Sparse Core Ops, SparseCore 0:
  17.3 40.9 all-gather.3
  64.5 26.5 reduce-scatter.1
  94.2 40.8 all-gather.5
